TPU v7x, 256 devices: a whole 4x4x8 slice. The times are simulated.
256 devices in a mesh: tg: 4 (over x), tc: 32 (over z, y), sp: 2 (over core).
Axes of the slice: x: 4, y: 4, z: 8, core: 2. Of those that a mesh axis runs over, the one named last changes fastest.
Arguments:
- initial: float32 [512, 128], P('sp'), may hold values from 0.5 to 1.5
- source: float32 [128, 512, 128], P(('tg', 'tc'), 'sp'), may hold values from -0.3 to 0.3
Outputs:
- c_values: float32 [128, 512, 128], P(('tg', 'tc'), 'sp')
- block_mean: float32 [128, 512, 128], P(('tg', 'tc'), 'sp')
All inputs are finite; a program needn't handle non-finite values.
Results may differ from a plain program's by a relative error of at most 0.00002.
Values sent between devices are 32-bit elements; how exact they have to be, the bound alone decides.
No kernel may reach another device: no remote copies, remote signals or barrier semaphores. Data moves between devices by JAX's collectives and lax.ppermute only.
A program may use at most 128 MiB of HBM per device.

v0:
```python
import jax
import jax.numpy as jnp
import numpy as np
from jax import lax
from jax.experimental import pallas as pl
from jax.experimental.pallas import tpu as pltpu
from jax.sharding import PartitionSpec as P

ROWS = 512
HALF = ROWS // 2
COLS = 128
LANES = COLS // 2
STEPS = 16
GROUP = 32
QUAD = 4

fine_center = 0.2
fine_behind = 0.25
fine_ahead = 0.15
coarse_center = 0.04
coarse_behind = 0.31
coarse_ahead = 0.17

HIGHEST = lax.Precision.HIGHEST

MESH_SHAPE = (4, 2, 2, 2, 4, 2)
MESH_AXES = ("x", "zh", "z1", "z0", "y", "sp")
PLANE = ("x", "z0", "y")
RUN = 8

GUESS, DEFECT, MEAN_STATE, MEAN_SOURCE, COARSE = 0, 1, 2, 3, 4
LAST_8, LAST_16, LAST_32 = 10, 11, 12
N_OPS = 13


def symbol(theta, phi, center, behind, ahead):
    return (
        center
        + behind * np.exp(-1j * theta)
        + ahead * np.exp(1j * theta)
        + behind * np.exp(-1j * phi)
        + ahead * np.exp(1j * phi)
    )


def operators(theta, phi):
    fine = symbol(theta, phi, fine_center, fine_behind, fine_ahead)
    coarse = symbol(theta, phi, coarse_center, coarse_behind, coarse_ahead)
    power, total = np.ones_like(fine), np.zeros_like(fine)
    inner_sum = np.zeros_like(fine)
    inner_power = np.zeros_like(fine)
    for step in range(STEPS):
        total = total + power
        if step < STEPS - 1:
            inner_sum = inner_sum + total
        power = power * fine
        if step < STEPS - 1:
            inner_power = inner_power + power
    found = [total, power, inner_power / (STEPS - 1), inner_sum / (STEPS - 1)]
    found += [coarse ** (1 << n) for n in range(6)]
    found += [power * coarse ** (n - 1) for n in (8, 16, 32)]
    return np.stack(found)


def slice_rows():
    core = np.arange(2)[:, None, None]
    q = np.arange(GROUP)[None, :, None]
    return 2 * (QUAD * q + np.arange(QUAD)[None, None, :]) + core


def mode_table():
    d = slice_rows()[..., None]
    lane = np.arange(COLS)
    row = np.where(lane > LANES, d + HALF, d)
    theta = 2 * np.pi * row / ROWS
    phi = np.where(lane == LANES, np.pi, 2 * np.pi * (lane % LANES) / COLS)
    value = operators(theta, phi + 0 * theta)
    on_u, on_v, across = value.real.copy(), value.real.copy(), value.imag.copy()
    for at, angle in ((0, 0.0), (LANES, np.pi)):
        on_u[:, 0, 0, 0, at] = operators(np.array(0.0), np.array(angle)).real
        on_v[:, 0, 0, 0, at] = operators(np.array(np.pi), np.array(angle)).real
        across[:, 0, 0, 0, at] = 0.0
    table = np.concatenate([on_u, on_v, -across, across], axis=3)
    table = np.moveaxis(table, 0, 2)
    return table.reshape(2, GROUP, 16 * N_OPS, COLS).astype(np.float32)


def row_table():
    turns = slice_rows()[..., None] * np.arange(HALF) % ROWS
    angle = 2 * np.pi * turns / ROWS
    table = np.concatenate([np.cos(angle), np.sin(angle)], axis=2)
    return table.reshape(2, HALF, HALF).astype(np.float32)


def column_tables():
    c = np.arange(COLS)[:, None]
    n = np.arange(LANES)[None, :]
    angle = 2 * np.pi * ((c * n) % COLS) / COLS
    forward = np.concatenate([np.cos(angle), -np.sin(angle)], 1)
    forward[:, LANES] = np.where(np.arange(COLS) % 2 == 0, 1.0, -1.0)
    backward = 2.0 * forward.T / (ROWS * COLS)
    return forward.astype(np.float32), backward.astype(np.float32)


def dot(a, b):
    return jnp.dot(a, b, precision=HIGHEST, preferred_element_type=jnp.float32)


def swap(x):
    return pltpu.roll(x, LANES, x.ndim - 1)


def flip(x):
    return pltpu.roll(x, QUAD, x.ndim - 2)


def tiles(x):
    return x.reshape(x.shape[0] // 8, 8, x.shape[1])


def iota(shape, dim):
    return lax.broadcasted_iota(jnp.int32, shape, dim)


def alternating(shape):
    return (1 - 2 * (iota(shape, 0) % 2)).astype(jnp.float32)


def parity():
    return (lax.axis_index("sp") + lax.axis_index("z1")) % 2


def prepare_kernel(src, init, rows, rows_t, table, src_o, init_o, rows_o, rows_t_o, table_o, sems):
    kind = parity()
    pairs = (
        (src, src_o),
        (rows.at[kind], rows_o),
        (init, init_o),
        (table.at[kind, own_slice()], table_o),
        (rows_t.at[kind], rows_t_o),
    )
    copies = [pltpu.make_async_copy(a, b, sems.at[n]) for n, (a, b) in enumerate(pairs)]
    for copy in copies:
        copy.start()
    for copy in copies:
        copy.wait()


def to_modes(product, first):
    a, b = tiles(product[:, :COLS]), tiles(product[:, COLS:])
    sub = iota(a.shape, 1)
    lane = iota(a.shape, 2)
    sign = jnp.where(sub < QUAD, 1.0, -1.0)
    own = sign * a
    b_flip = flip(b)
    result = jnp.where(lane < LANES, own + swap(flip(a)), swap(sign * b) + b_flip)
    edge = lane % LANES == 0
    zero_mode = jnp.logical_and(first, jnp.logical_and(iota(a.shape, 0) == 0, sub == QUAD))
    result = jnp.where(edge, jnp.where(zero_mode, b_flip, own), result)
    return result.reshape(product.shape[0], COLS)


def own_slice():
    return lax.axis_index("x") * 8 + lax.axis_index("z0") * 4 + lax.axis_index("y")


def fold(own, other):
    odd, lower = parity() == 1, lax.axis_index("sp") == 1
    own_sign = jnp.where(jnp.logical_and(odd, lower), -1.0, 1.0)
    other_sign = jnp.where(jnp.logical_and(odd, jnp.logical_not(lower)), -1.0, 1.0)
    return own_sign * own[...] + other_sign * other[...]


def columns(folded, col):
    y = dot(folded, col[...])
    return jnp.concatenate([y, y * alternating(y.shape)], axis=1)


def forward_kernel(src, src_other, init, init_other, col, rows, out, init_out):
    first = parity() == 0
    out[...] = to_modes(dot(rows[...], columns(fold(src, src_other), col)), first)
    init_out[...] = fold(init, init_other)


def initial_kernel(folded, col, rows, out):
    at = own_slice()
    own_rows = rows[pl.ds(pl.multiple_of(8 * at, 8), 8), :]
    first = jnp.logical_and(parity() == 0, at == 0)
    out[...] = to_modes(dot(own_rows, columns(folded[...], col)), first)


class Operators:
    def __init__(self, table):
        self.table = table

    def __call__(self, n, x):
        itself, partner = (self.table[16 * n + j : 16 * n + j + 8] for j in (0, 8))
        return itself * x + partner * flip(x)


def after(first, rest):
    return jnp.concatenate([first, rest], axis=1)


def place():
    return 2 * lax.axis_index("zh") + lax.axis_index("z1")


def scan_kernel(got, table, c_out, mean_out, message):
    op = Operators(table)
    f = got[...].reshape(4, RUN, 8, COLS)
    w = op(GUESS, f)
    t = w
    for level in range(3):
        d = 1 << level
        t = after(t[:, :d], t[:, d:] + op(COARSE + level, t[:, :-d]))
    c = after(w[:, :1], w[:, 1:] + op(DEFECT, t[:, :-1]))
    source_part = op(MEAN_SOURCE, f)
    c_out[...] = c
    mean_out[...] = after(source_part[:, :1], source_part[:, 1:] + op(MEAN_STATE, c[:, :-1]))
    message[0] = t[:, RUN - 1]
    message[1] = c[:, RUN - 1]


def join_kernel(own, other, table, message, kept):
    op = Operators(table)
    later = lax.axis_index("z1") == 1
    mine, theirs = own[0], other[0]
    prefix = jnp.where(later, theirs, 0.0)
    low = jnp.where(later, theirs, mine)
    high = jnp.where(later, mine, theirs)
    message[0] = op(COARSE + 3, low) + high
    message[1] = own[1] + op(LAST_8, prefix)
    kept[0] = prefix
    kept[1] = jnp.where(later, other[1], 0.0)


def finish_kernel(c_in, mean_in, kept, own, other, init, table, out):
    op = Operators(table)
    at = place()
    second = at >= 2
    at_start = at % 2 == 0
    mine, theirs, theirs_c = own[0], other[0], other[1]
    low = jnp.where(second, theirs, mine)
    high = jnp.where(second, mine, theirs)
    total = op(COARSE + 4, low) + high
    state = [init[...]]
    for x in range(3):
        state.append(op(COARSE + 5, state[x]) + total[x])
    state = jnp.stack(state)
    part = jnp.where(second, low, 0.0)
    part_c = jnp.where(second, theirs_c, 0.0)
    carry = kept[0] + jnp.where(at_start, part, op(COARSE + 3, part))
    before = kept[1] + jnp.where(at_start, part_c, op(LAST_8, part))
    by_8, by_16 = op(COARSE + 3, state), op(COARSE + 4, state)
    by_24 = op(COARSE + 3, by_16)
    carry = carry + jnp.where(
        at == 0, state, jnp.where(at == 1, by_8, jnp.where(at == 2, by_16, by_24))
    )
    to_last = jnp.where(at == 1, state, jnp.where(at == 2, by_8, by_16))
    before = before + op(LAST_8, to_last)
    ends = theirs_c[:3] + op(LAST_16, low[:3]) + op(LAST_32, state[:3])
    before = jnp.where(at == 0, jnp.concatenate([init[...][None], ends], axis=0), before)
    spread = carry[:, None]
    for level in range(3):
        spread = after(spread, op(COARSE + level, spread))
    added = op(DEFECT, spread)
    shift = after(before[:, None], added[:, :-1])
    c = c_in[...] + added
    mean = mean_in[...] + op(MEAN_STATE, shift)
    out[:, :8] = c.reshape(GROUP, 8, COLS)
    out[:, 8:] = mean.reshape(GROUP, 8, COLS)


def backward_kernel(got, rows_t, col, out, own_out):
    odd, lower = parity() == 1, lax.axis_index("sp") == 1
    got_v = got[...]
    parts = [got_v[:, :8], got_v[:, 8:]]
    sub = iota(parts[0].shape, 1)
    flat = lambda v: v.reshape(HALF, COLS)
    left = [flat(jnp.where(sub < QUAD, v, -v)) for v in parts]
    right = [flat(flip(v)) for v in parts]
    product = dot(rows_t[...], jnp.concatenate(left + right, axis=1))
    sign = alternating((HALF, COLS))
    lane = iota((HALF, COLS), 1)
    own_sign = jnp.where(jnp.logical_and(odd, lower), -1.0, 1.0)
    sent_sign = jnp.where(jnp.logical_and(odd, jnp.logical_not(lower)), -1.0, 1.0)
    zero_mode = jnp.where(odd, 0.0, 0.5)
    for n, v in enumerate(parts):
        e = product[:, COLS * n : COLS * (n + 1)]
        f = product[:, COLS * (n + 2) : COLS * (n + 3)]
        y = jnp.where(lane < LANES, e + sign * swap(e), swap(f) + sign * f)
        first_u, first_v = v[0, :1], v[0, QUAD : QUAD + 1]
        edge = e + zero_mode * (sign * first_v - first_u)
        part = dot(jnp.where(lane % LANES == 0, edge, y), col[...])
        out[n] = sent_sign * part
        own_out[n] = own_sign * part


PARAMS = pltpu.CompilerParams(vmem_limit_bytes=32 * 1024 * 1024)


def call(kernel, shapes, args, hbm=False, scratch=()):
    space = pltpu.HBM if hbm else pltpu.VMEM
    return pl.pallas_call(
        kernel,
        out_shape=[jax.ShapeDtypeStruct(s, jnp.float32) for s in shapes],
        in_specs=[pl.BlockSpec(memory_space=space)] * len(args),
        out_specs=[pl.BlockSpec(memory_space=pltpu.VMEM)] * len(shapes),
        scratch_shapes=scratch,
        compiler_params=PARAMS,
    )(*args)


def shards(initial, source):
    rows = row_table()
    forward, backward = column_tables()
    own = source[0]
    swap_two = [(0, 1), (1, 0)]
    src_other = lax.ppermute(own, "sp", swap_two)
    init_other = lax.ppermute(initial, "sp", swap_two)
    block = (HALF, COLS)
    square = (HALF, HALF)
    constants = [rows, rows.transpose(0, 2, 1).copy(), mode_table()]
    args = [own, initial, *(jnp.asarray(a) for a in constants)]
    src, init, rows_v, rows_t_v, table = call(
        prepare_kernel,
        [block, block, square, square, (16 * N_OPS, COLS)],
        [pltpu.with_memory_space_constraint(a, pltpu.HBM) for a in args],
        hbm=True,
        scratch=[pltpu.SemaphoreType.DMA((5,))],
    )
    sent, folded = call(
        forward_kernel, [block, block], [src, src_other, init, init_other, forward, rows_v]
    )
    got = lax.all_to_all(sent.reshape(GROUP, 8, COLS), PLANE, 0, 0, tiled=True)
    runs, ends = (4, RUN, 8, COLS), (2, 4, 8, COLS)
    c, mean, message = call(scan_kernel, [runs, runs, ends], [got, table])
    folded, message = lax.optimization_barrier((folded, message))
    other = lax.ppermute(message, ("z1", "sp"), [(i, i ^ 3) for i in range(4)])
    (init_modes,) = call(initial_kernel, [(8, COLS)], [folded, forward, rows_v])
    message, kept = call(join_kernel, [ends, ends], [message, other, table])
    other = lax.ppermute(message, ("zh", "z1", "sp"), [(i, i ^ 7) for i in range(8)])
    (back,) = call(
        finish_kernel,
        [(GROUP, 16, COLS)],
        [c, mean, kept, message, other, init_modes, table],
    )
    modes = lax.all_to_all(back, PLANE, 0, 0, tiled=True)
    part, own_part = call(
        backward_kernel, [(2, HALF, COLS), (2, HALF, COLS)], [modes, rows_t_v, backward]
    )
    other_part = lax.ppermute(part, "sp", swap_two)
    return own_part[:1] + other_part[:1], own_part[1:] + other_part[1:]


def solution(mesh):
    mesh = jax.sharding.Mesh(mesh.devices.reshape(MESH_SHAPE), MESH_AXES)
    by_block = P(MESH_AXES[:-1], "sp", None)
    return jax.shard_map(
        shards,
        mesh=mesh,
        in_specs=(P("sp", None), by_block),
        out_specs=(by_block, by_block),
        check_vma=False,
    )
```

profile of v0, /device:TPU:1, one launch (start us, length us, event | category | flops | bytes accessed | tf_op | source)
XLA Modules:
  0.0 49.2 jit_solution(493798265747138662)
XLA Ops:
  0.6 0.0 copy-start
  0.6 0.0 copy-start.1
  0.7 3.3 %collective-permute-start = (f32[256,128]{1,0:T(8,128)}, f32[256,128]{1,0:T(8,128)S(1)}, u32[]{:S(2)}, u32[]{:S(2)}) collective-permute-start(f32[256,128]{1,0:T(8,128)} %bitcast.3), channel_id=1, source_target_pairs={{0,1},{1,0},{2,3},{3,2},{4,5},{5,4},{6,7},{7,6},{8,9},{9,8},{10,11... | collective-permute-start | bytes 393224 | tf_op jit(solution)/shard_map/ppermute | solution.py:320
  4.0 0.1 collective-permute-start.1
  4.1 1.2 %shard_map.86 = (f32[256,128]{1,0:T(8,128)S(1)}, f32[256,128]{1,0:T(8,128)S(1)}, f32[256,256]{1,0:T(8,128)S(1)}, f32[256,256]{1,0:T(8,128)S(1)}, f32[208,128]{1,0:T(8,128)S(1)}) custom-call(f32[256,128]{1,0:T(8,128)} %bitcast.4, f32[256,128]{1,0:T(8,128)} %init.1, f32[2,256,256]{2,1,0:T(8,128)} %constant.10.clone.rows, ...), custom_call_target="tpu_custom_call" | custom-call | tf_op jit(solution)/shard_map/pallas_call | solution.py:305
  5.3 0.0 collective-permute-done.src_other
  5.3 0.2 collective-permute-done.1.init_other
  5.5 0.0 copy-done
  5.5 0.9 %shard_map.87 = (f32[256,128]{1,0:T(8,128)S(1)}, f32[256,128]{1,0:T(8,128)S(1)}) custom-call(f32[256,128]{1,0:T(8,128)S(1)} %get-tuple-element.18.src, f32[256,128]{1,0:T(8,128)S(1)} %collective-permute-done.src_other, f32[256,128]{1,0:T(8,128)S(1)} %get-tuple-element.19.init, f32[256,128]{1,0:T(8,128)S(1)} %collective-permute-done.1.init_other, ...), custom_call_target="tpu_custom_call" | custom-call | tf_op jit(solution)/shard_map/pallas_call | solution.py:305
  6.4 14.0 %all_to_all.10.got = f32[32,8,128]{2,1,0:T(8,128)S(1)} all-to-all(f32[32,8,128]{2,1,0:T(8,128)S(1)} %bitcast.2), channel_id=1, replica_groups=mesh['x'=4,'zh'=2,'z1'=2,'z0'=2,'y'=4,'sp'=2] {'x','z0','y'}, dimensions={0} | all-to-all | bytes 262144 | tf_op jit(solution)/shard_map/all_to_all | solution.py:336
  20.4 0.1 shard_map.88
  20.5 4.6 %collective-permute-start.2 = (f32[2,4,8,128]{3,2,1,0:T(8,128)S(1)}, f32[2,4,8,128]{3,2,1,0:T(8,128)S(1)}, u32[]{:S(2)}, u32[]{:S(2)}) collective-permute-start(f32[2,4,8,128]{3,2,1,0:T(8,128)S(1)} %get-tuple-element.27.own), channel_id=1, source_target_pairs={{0,17},{1,16},{16,1},{17,0},{2,19},{3,18},{18,3},{19,2},{4,21},{5,... | collective-permute-start | bytes 98312 | tf_op jit(solution)/shard_map/ppermute | solution.py:340
  25.2 2.0 %collective-permute-done.2.other = f32[2,4,8,128]{3,2,1,0:T(8,128)S(1)} collective-permute-done((f32[2,4,8,128]{3,2,1,0:T(8,128)S(1)}, f32[2,4,8,128]{3,2,1,0:T(8,128)S(1)}, u32[]{:S(2)}, u32[]{:S(2)}) %collective-permute-start.2) | collective-permute-done | bytes 32800 | tf_op jit(solution)/shard_map/ppermute | solution.py:340
  27.1 4.5 %collective-permute-start.3 = (f32[2,4,8,128]{3,2,1,0:T(8,128)S(1)}, f32[2,4,8,128]{3,2,1,0:T(8,128)S(1)}, u32[]{:S(2)}, u32[]{:S(2)}) collective-permute-start(f32[2,4,8,128]{3,2,1,0:T(8,128)S(1)} %get-tuple-element.29.own), channel_id=1, source_target_pairs={{0,49},{1,48},{16,33},{17,32},{32,17},{33,16},{48,1},{49,0},{2,51}... | collective-permute-start | bytes 98312 | tf_op jit(solution)/shard_map/ppermute | solution.py:343
  31.6 0.7 %shard_map.90.init = f32[8,128]{1,0:T(8,128)S(1)} custom-call(f32[256,128]{1,0:T(8,128)S(1)} %get-tuple-element.30.folded, f32[128,128]{1,0:T(8,128)S(1)} %copy-done, f32[256,256]{1,0:T(8,128)S(1)} %get-tuple-element.20.rows), custom_call_target="tpu_custom_call" | custom-call | tf_op jit(solution)/shard_map/pallas_call | solution.py:305
  32.3 0.9 %collective-permute-done.3.other = f32[2,4,8,128]{3,2,1,0:T(8,128)S(1)} collective-permute-done((f32[2,4,8,128]{3,2,1,0:T(8,128)S(1)}, f32[2,4,8,128]{3,2,1,0:T(8,128)S(1)}, u32[]{:S(2)}, u32[]{:S(2)}) %collective-permute-start.3) | collective-permute-done | bytes 32800 | tf_op jit(solution)/shard_map/ppermute | solution.py:343
  33.2 0.1 shard_map.91
  33.3 12.4 %all_to_all.11.got = f32[32,16,128]{2,1,0:T(8,128)S(1)} all-to-all(f32[32,16,128]{2,1,0:T(8,128)S(1)} %shard_map.91), channel_id=1, replica_groups=mesh['x'=4,'zh'=2,'z1'=2,'z0'=2,'y'=4,'sp'=2] {'x','z0','y'}, dimensions={0} | all-to-all | bytes 524288 | tf_op jit(solution)/shard_map/all_to_all | solution.py:349
  45.8 0.0 copy-done.1
  45.8 1.1 %shard_map.92 = (f32[2,256,128]{2,1,0:T(8,128)S(1)}, f32[2,256,128]{2,1,0:T(8,128)S(1)}) custom-call(f32[32,16,128]{2,1,0:T(8,128)S(1)} %all_to_all.11.got, f32[256,256]{1,0:T(8,128)S(1)} %get-tuple-element.31.rows_t, f32[128,128]{1,0:T(8,128)S(1)} %copy-done.1), custom_call_target="tpu_custom_call" | custom-call | tf_op jit(solution)/shard_map/pallas_call | solution.py:305
  46.9 0.1 collective-permute-start.4
  47.0 1.5 %collective-permute-done.4 = f32[2,256,128]{2,1,0:T(8,128)S(1)} collective-permute-done((f32[2,256,128]{2,1,0:T(8,128)S(1)}, f32[2,256,128]{2,1,0:T(8,128)S(1)}, u32[]{:S(2)}, u32[]{:S(2)}) %collective-permute-start.4) | collective-permute-done | bytes 262176 | tf_op jit(solution)/shard_map/ppermute | solution.py:353
  48.5 0.7 %slice_add_fusion = (f32[1,256,128]{2,1,0:T(8,128)}, f32[1,256,128]{2,1,0:T(8,128)}) fusion(f32[2,256,128]{2,1,0:T(8,128)S(1)} %collective-permute-done.4, f32[2,256,128]{2,1,0:T(8,128)S(1)} %get-tuple-element.32), kind=kLoop, calls=%fused_computation | loop fusion | flops 65536 | bytes 786432 | tf_op jit(solution)/shard_map/add | solution.py:354
  (1 shorter events, 0.0 us)
Async XLA Ops:
  0.6 4.9 %copy-start = (f32[128,128]{1,0:T(8,128)S(1)}, f32[128,128]{1,0:T(8,128)}, u32[]{:S(2)}) copy-start(f32[128,128]{1,0:T(8,128)} %constant.13.clone.col) | copy-start | bytes 196612
  0.6 45.1 %copy-start.1 = (f32[128,128]{1,0:T(8,128)S(1)}, f32[128,128]{1,0:T(8,128)}, u32[]{:S(2)}) copy-start(f32[128,128]{1,0:T(8,128)} %constant.14.clone.col) | copy-start | bytes 196612
  0.7 4.7 %collective-permute-start = (f32[256,128]{1,0:T(8,128)}, f32[256,128]{1,0:T(8,128)S(1)}, u32[]{:S(2)}, u32[]{:S(2)}) collective-permute-start(f32[256,128]{1,0:T(8,128)} %bitcast.3), channel_id=1, source_target_pairs={{0,1},{1,0},{2,3},{3,2},{4,5},{5,4},{6,7},{7,6},{8,9},{9,8},{10,11... | collective-permute-start | bytes 393224 | tf_op jit(solution)/shard_map/ppermute | solution.py:320
  4.0 1.6 %collective-permute-start.1 = (f32[256,128]{1,0:T(8,128)}, f32[256,128]{1,0:T(8,128)S(1)}, u32[]{:S(2)}, u32[]{:S(2)}) collective-permute-start(f32[256,128]{1,0:T(8,128)} %init.1), channel_id=1, source_target_pairs={{0,1},{1,0},{2,3},{3,2},{4,5},{5,4},{6,7},{7,6},{8,9},{9,8},{10,11... | collective-permute-start | bytes 393224 | tf_op jit(solution)/shard_map/ppermute | solution.py:321
  20.5 6.6 %collective-permute-start.2 = (f32[2,4,8,128]{3,2,1,0:T(8,128)S(1)}, f32[2,4,8,128]{3,2,1,0:T(8,128)S(1)}, u32[]{:S(2)}, u32[]{:S(2)}) collective-permute-start(f32[2,4,8,128]{3,2,1,0:T(8,128)S(1)} %get-tuple-element.27.own), channel_id=1, source_target_pairs={{0,17},{1,16},{16,1},{17,0},{2,19},{3,18},{18,3},{19,2},{4,21},{5,... | collective-permute-start | bytes 98312 | tf_op jit(solution)/shard_map/ppermute | solution.py:340
  27.1 6.1 %collective-permute-start.3 = (f32[2,4,8,128]{3,2,1,0:T(8,128)S(1)}, f32[2,4,8,128]{3,2,1,0:T(8,128)S(1)}, u32[]{:S(2)}, u32[]{:S(2)}) collective-permute-start(f32[2,4,8,128]{3,2,1,0:T(8,128)S(1)} %get-tuple-element.29.own), channel_id=1, source_target_pairs={{0,49},{1,48},{16,33},{17,32},{32,17},{33,16},{48,1},{49,0},{2,51}... | collective-permute-start | bytes 98312 | tf_op jit(solution)/shard_map/ppermute | solution.py:343
  46.9 1.6 %collective-permute-start.4 = (f32[2,256,128]{2,1,0:T(8,128)S(1)}, f32[2,256,128]{2,1,0:T(8,128)S(1)}, u32[]{:S(2)}, u32[]{:S(2)}) collective-permute-start(f32[2,256,128]{2,1,0:T(8,128)S(1)} %get-tuple-element.33), channel_id=1, source_target_pairs={{0,1},{1,0},{2,3},{3,2},{4,5},{5,4},{6,7},{7,6},{8,9},{9,8},{10,11... | collective-permute-start | bytes 786440 | tf_op jit(solution)/shard_map/ppermute | solution.py:353
where the time goes:
time: 49.4 us; the launch traced here: 49.2 us
  blocking collectives  26.4 us (53%)
  starting transfers between devices  12.6 us (26%)
  waiting for transfers between devices  4.59 us (9%)
  Pallas kernels  4.09 us (8%)
  other arithmetic  0.73 us (1%)
  between operations  0.7 us (1%)
    all_to_all x1, blocking collectives, shards(): got = lax.all_to_all(sent.reshape(GROUP, 8, COLS), PLANE, 0, 0, tiled=True)  14 us
    all_to_all x1, blocking collectives, shards(): modes = lax.all_to_all(back, PLANE, 0, 0, tiled=True)  12.4 us
    ppermute x1, starting transfers between devices, shards(): other = lax.ppermute(message, ('z1', 'sp'), [(i, i ^ 3) for i in range(4)])  4.62 us
    ppermute x1, starting transfers between devices, shards(): lax.ppermute(message, ('zh', 'z1', 'sp'), [(i, i ^ 7) for i in range(8)])  4.51 us
    pallas_call x7, Pallas kernels, call(): pl.pallas_call(kernel, out_shape=[jax.ShapeDtypeStruct(s, jnp.float32) fo...  4.09 us
    ppermute x1, starting transfers between devices, shards(): src_other = lax.ppermute(own, 'sp', swap_two)  3.33 us
    ppermute x1, waiting for transfers between devices, shards(): other = lax.ppermute(message, ('z1', 'sp'), [(i, i ^ 3) for i in range(4)])  1.95 us
    ppermute x1, waiting for transfers between devices, shards(): other_part = lax.ppermute(part, 'sp', swap_two)  1.52 us
  transfers between devices with their start and end apart: 5, of which 4 were waited for; matrix products, arithmetic and copies ran while one was open for 0% of the time, Pallas kernels for 4%

commit v1 on v0

--- a/solution.py
+++ b/solution.py
@@ -106,6 +106,17 @@
     return jnp.dot(a, b, precision=HIGHEST, preferred_element_type=jnp.float32)
 
 
+def halves(x):
+    high = x.astype(jnp.bfloat16)
+    return high, (x - high.astype(jnp.float32)).astype(jnp.bfloat16)
+
+
+def dot_split(a, b):
+    (ah, al), (bh, bl) = halves(a), halves(b)
+    one = lambda x, y: jnp.dot(x, y, preferred_element_type=jnp.float32)
+    return one(ah, bh) + (one(ah, bl) + one(al, bh))
+
+
 def swap(x):
     return pltpu.roll(x, LANES, x.ndim - 1)
 
@@ -176,17 +187,18 @@
     return jnp.concatenate([y, y * alternating(y.shape)], axis=1)
 
 
-def forward_kernel(src, src_other, init, init_other, col, rows, out, init_out):
+def forward_kernel(src, src_other, col, rows, out):
     first = parity() == 0
     out[...] = to_modes(dot(rows[...], columns(fold(src, src_other), col)), first)
-    init_out[...] = fold(init, init_other)
-
-
-def initial_kernel(folded, col, rows, out):
+
+
+def initial_kernel(init, col, rows, out):
     at = own_slice()
     own_rows = rows[pl.ds(pl.multiple_of(8 * at, 8), 8), :]
     first = jnp.logical_and(parity() == 0, at == 0)
-    out[...] = to_modes(dot(own_rows, columns(folded[...], col)), first)
+    part = to_modes(dot(own_rows, columns(init[...], col)), first)
+    odd, lower = parity() == 1, lax.axis_index("sp") == 1
+    out[...] = jnp.where(jnp.logical_and(odd, lower), -1.0, 1.0) * part
 
 
 class Operators:
@@ -222,29 +234,31 @@
     message[1] = c[:, RUN - 1]
 
 
-def join_kernel(own, other, table, message, kept):
+def join_kernel(own, other, init, table, message, kept):
     op = Operators(table)
     later = lax.axis_index("z1") == 1
     mine, theirs = own[0], other[0]
     prefix = jnp.where(later, theirs, 0.0)
     low = jnp.where(later, theirs, mine)
     high = jnp.where(later, mine, theirs)
-    message[0] = op(COARSE + 3, low) + high
-    message[1] = own[1] + op(LAST_8, prefix)
+    message[:4] = op(COARSE + 3, low) + high
+    message[4:8] = own[1] + op(LAST_8, prefix)
+    message[8] = init[...]
     kept[0] = prefix
     kept[1] = jnp.where(later, other[1], 0.0)
 
 
-def finish_kernel(c_in, mean_in, kept, own, other, init, table, out):
+def finish_kernel(c_in, mean_in, kept, own, other, table, out):
     op = Operators(table)
     at = place()
     second = at >= 2
     at_start = at % 2 == 0
-    mine, theirs, theirs_c = own[0], other[0], other[1]
+    mine, theirs, theirs_c = own[:4], other[:4], other[4:8]
+    init = own[8] + other[8]
     low = jnp.where(second, theirs, mine)
     high = jnp.where(second, mine, theirs)
     total = op(COARSE + 4, low) + high
-    state = [init[...]]
+    state = [init]
     for x in range(3):
         state.append(op(COARSE + 5, state[x]) + total[x])
     state = jnp.stack(state)
@@ -260,7 +274,7 @@
     to_last = jnp.where(at == 1, state, jnp.where(at == 2, by_8, by_16))
     before = before + op(LAST_8, to_last)
     ends = theirs_c[:3] + op(LAST_16, low[:3]) + op(LAST_32, state[:3])
-    before = jnp.where(at == 0, jnp.concatenate([init[...][None], ends], axis=0), before)
+    before = jnp.where(at == 0, jnp.concatenate([init[None], ends], axis=0), before)
     spread = carry[:, None]
     for level in range(3):
         spread = after(spread, op(COARSE + level, spread))
@@ -276,11 +290,16 @@
     odd, lower = parity() == 1, lax.axis_index("sp") == 1
     got_v = got[...]
     parts = [got_v[:, :8], got_v[:, 8:]]
-    sub = iota(parts[0].shape, 1)
+    shape = parts[0].shape
+    sub = iota(shape, 1)
+    origin = jnp.logical_and(iota(shape, 0) == 0, jnp.logical_and(sub == 0, iota(shape, 2) == 0))
+    origin = jnp.logical_and(origin, jnp.logical_not(odd))
+    constants = [jnp.where(odd, 0.0, v[0, :1, :1] * (1.0 / (ROWS * COLS))) for v in parts]
+    parts = [jnp.where(origin, 0.0, v) for v in parts]
     flat = lambda v: v.reshape(HALF, COLS)
     left = [flat(jnp.where(sub < QUAD, v, -v)) for v in parts]
     right = [flat(flip(v)) for v in parts]
-    product = dot(rows_t[...], jnp.concatenate(left + right, axis=1))
+    product = dot_split(rows_t[...], jnp.concatenate(left + right, axis=1))
     sign = alternating((HALF, COLS))
     lane = iota((HALF, COLS), 1)
     own_sign = jnp.where(jnp.logical_and(odd, lower), -1.0, 1.0)
@@ -292,7 +311,7 @@
         y = jnp.where(lane < LANES, e + sign * swap(e), swap(f) + sign * f)
         first_u, first_v = v[0, :1], v[0, QUAD : QUAD + 1]
         edge = e + zero_mode * (sign * first_v - first_u)
-        part = dot(jnp.where(lane % LANES == 0, edge, y), col[...])
+        part = dot_split(jnp.where(lane % LANES == 0, edge, y), col[...]) + constants[n]
         out[n] = sent_sign * part
         own_out[n] = own_sign * part
 
@@ -318,7 +337,6 @@
     own = source[0]
     swap_two = [(0, 1), (1, 0)]
     src_other = lax.ppermute(own, "sp", swap_two)
-    init_other = lax.ppermute(initial, "sp", swap_two)
     block = (HALF, COLS)
     square = (HALF, HALF)
     constants = [rows, rows.transpose(0, 2, 1).copy(), mode_table()]
@@ -330,21 +348,21 @@
         hbm=True,
         scratch=[pltpu.SemaphoreType.DMA((5,))],
     )
-    sent, folded = call(
-        forward_kernel, [block, block], [src, src_other, init, init_other, forward, rows_v]
-    )
+    (sent,) = call(forward_kernel, [block], [src, src_other, forward, rows_v])
     got = lax.all_to_all(sent.reshape(GROUP, 8, COLS), PLANE, 0, 0, tiled=True)
     runs, ends = (4, RUN, 8, COLS), (2, 4, 8, COLS)
     c, mean, message = call(scan_kernel, [runs, runs, ends], [got, table])
-    folded, message = lax.optimization_barrier((folded, message))
+    init, message = lax.optimization_barrier((init, message))
     other = lax.ppermute(message, ("z1", "sp"), [(i, i ^ 3) for i in range(4)])
-    (init_modes,) = call(initial_kernel, [(8, COLS)], [folded, forward, rows_v])
-    message, kept = call(join_kernel, [ends, ends], [message, other, table])
+    (init_part,) = call(initial_kernel, [(8, COLS)], [init, forward, rows_v])
+    message, kept = call(
+        join_kernel, [(9, 8, COLS), ends], [message, other, init_part, table]
+    )
     other = lax.ppermute(message, ("zh", "z1", "sp"), [(i, i ^ 7) for i in range(8)])
     (back,) = call(
         finish_kernel,
         [(GROUP, 16, COLS)],
-        [c, mean, kept, message, other, init_modes, table],
+        [c, mean, kept, message, other, table],
     )
     modes = lax.all_to_all(back, PLANE, 0, 0, tiled=True)
     part, own_part = call(

time: 49.4 us -> 48.6 us (0.984)
    ppermute x1, waiting for transfers between devices: 0.91 us -> 1.64 us  [shards(): lax.ppermute(message, ('zh', 'z1', 'sp'), [(i, i ^ 7) for i in range(8)])]
    ppermute x1, waiting for transfers between devices: 1.95 us -> 1.26 us  [shards(): other = lax.ppermute(message, ('z1', 'sp'), [(i, i ^ 3) for i in range(4)])]
  transfers between devices with their start and end apart: 5 -> 4, of which waited for: 4 -> 3; matrix products, arithmetic and copies ran while one was open for 0% -> 0% of each run, Pallas kernels for 4% -> 4%
where the time goes in v1:
time: 48.6 us; the launch traced here: 48.4 us
  blocking collectives  26.2 us (54%)
  starting transfers between devices  12.7 us (26%)
  waiting for transfers between devices  4.34 us (9%)
  Pallas kernels  3.76 us (8%)
  other arithmetic  0.74 us (2%)
  between operations  0.7 us (1%)
    all_to_all x1, blocking collectives, shards(): got = lax.all_to_all(sent.reshape(GROUP, 8, COLS), PLANE, 0, 0, tiled=True)  14 us
    all_to_all x1, blocking collectives, shards(): modes = lax.all_to_all(back, PLANE, 0, 0, tiled=True)  12.2 us
    ppermute x1, starting transfers between devices, shards(): other = lax.ppermute(message, ('z1', 'sp'), [(i, i ^ 3) for i in range(4)])  4.67 us
    ppermute x1, starting transfers between devices, shards(): lax.ppermute(message, ('zh', 'z1', 'sp'), [(i, i ^ 7) for i in range(8)])  4.5 us
    pallas_call x7, Pallas kernels, call(): pl.pallas_call(kernel, out_shape=[jax.ShapeDtypeStruct(s, jnp.float32) fo...  3.76 us
    ppermute x1, starting transfers between devices, shards(): src_other = lax.ppermute(own, 'sp', swap_two)  3.33 us
    ppermute x1, waiting for transfers between devices, shards(): lax.ppermute(message, ('zh', 'z1', 'sp'), [(i, i ^ 7) for i in range(8)])  1.64 us
    ppermute x1, waiting for transfers between devices, shards(): other_part = lax.ppermute(part, 'sp', swap_two)  1.43 us
  transfers between devices with their start and end apart: 4, of which 3 were waited for; matrix products, arithmetic and copies ran while one was open for 0% of the time, Pallas kernels for 4%

profile of v1, /device:TPU:1, one launch (start us, length us, event | category | flops | bytes accessed | tf_op | source)
XLA Modules:
  0.0 48.4 jit_solution(1729625363897054049)
XLA Ops:
  0.6 0.0 copy-start
  0.6 0.0 copy-start.1
  0.7 3.3 %collective-permute-start = (f32[256,128]{1,0:T(8,128)}, f32[256,128]{1,0:T(8,128)S(1)}, u32[]{:S(2)}, u32[]{:S(2)}) collective-permute-start(f32[256,128]{1,0:T(8,128)} %bitcast.3), channel_id=1, source_target_pairs={{0,1},{1,0},{2,3},{3,2},{4,5},{5,4},{6,7},{7,6},{8,9},{9,8},{10,11... | collective-permute-start | bytes 393224 | tf_op jit(solution)/shard_map/ppermute | solution.py:339
  4.0 1.2 %shard_map.86 = (f32[256,128]{1,0:T(8,128)S(1)}, f32[256,128]{1,0:T(8,128)S(1)}, f32[256,256]{1,0:T(8,128)S(1)}, f32[256,256]{1,0:T(8,128)S(1)}, f32[208,128]{1,0:T(8,128)S(1)}) custom-call(f32[256,128]{1,0:T(8,128)} %bitcast.4, f32[256,128]{1,0:T(8,128)} %init.1, f32[2,256,256]{2,1,0:T(8,128)} %constant.10.clone.rows, ...), custom_call_target="tpu_custom_call" | custom-call | tf_op jit(solution)/shard_map/pallas_call | solution.py:324
  5.2 0.0 collective-permute-done.src_other
  5.2 0.0 copy-done
  5.2 0.9 %shard_map.87 = f32[256,128]{1,0:T(8,128)S(1)} custom-call(f32[256,128]{1,0:T(8,128)S(1)} %get-tuple-element.16.src, f32[256,128]{1,0:T(8,128)S(1)} %collective-permute-done.src_other, f32[128,128]{1,0:T(8,128)S(1)} %copy-done, f32[256,256]{1,0:T(8,128)S(1)} %get-tuple-element.17.rows), custom_call_target="tpu_custom_call" | custom-call | tf_op jit(solution)/shard_map/pallas_call | solution.py:324
  6.1 14.0 %all_to_all.10.got = f32[32,8,128]{2,1,0:T(8,128)S(1)} all-to-all(f32[32,8,128]{2,1,0:T(8,128)S(1)} %bitcast.2), channel_id=1, replica_groups=mesh['x'=4,'zh'=2,'z1'=2,'z0'=2,'y'=4,'sp'=2] {'x','z0','y'}, dimensions={0} | all-to-all | bytes 262144 | tf_op jit(solution)/shard_map/all_to_all | solution.py:352
  20.2 0.1 shard_map.88
  20.3 4.7 %collective-permute-start.1 = (f32[2,4,8,128]{3,2,1,0:T(8,128)S(1)}, f32[2,4,8,128]{3,2,1,0:T(8,128)S(1)}, u32[]{:S(2)}, u32[]{:S(2)}) collective-permute-start(f32[2,4,8,128]{3,2,1,0:T(8,128)S(1)} %get-tuple-element.23.own), channel_id=1, source_target_pairs={{0,17},{1,16},{16,1},{17,0},{2,19},{3,18},{18,3},{19,2},{4,21},{5,... | collective-permute-start | bytes 98312 | tf_op jit(solution)/shard_map/ppermute | solution.py:356
  24.9 0.7 %shard_map.89.init = f32[8,128]{1,0:T(8,128)S(1)} custom-call(f32[256,128]{1,0:T(8,128)S(1)} %get-tuple-element.24.init, f32[128,128]{1,0:T(8,128)S(1)} %copy-done, f32[256,256]{1,0:T(8,128)S(1)} %get-tuple-element.17.rows), custom_call_target="tpu_custom_call" | custom-call | tf_op jit(solution)/shard_map/pallas_call | solution.py:324
  25.6 1.3 %collective-permute-done.1.other = f32[2,4,8,128]{3,2,1,0:T(8,128)S(1)} collective-permute-done((f32[2,4,8,128]{3,2,1,0:T(8,128)S(1)}, f32[2,4,8,128]{3,2,1,0:T(8,128)S(1)}, u32[]{:S(2)}, u32[]{:S(2)}) %collective-permute-start.1) | collective-permute-done | bytes 32800 | tf_op jit(solution)/shard_map/ppermute | solution.py:356
  26.9 4.5 %collective-permute-start.2 = (f32[9,8,128]{2,1,0:T(8,128)S(1)}, f32[9,8,128]{2,1,0:T(8,128)S(1)}, u32[]{:S(2)}, u32[]{:S(2)}) collective-permute-start(f32[9,8,128]{2,1,0:T(8,128)S(1)} %get-tuple-element.26.own), channel_id=1, source_target_pairs={{0,49},{1,48},{16,33},{17,32},{32,17},{33,16},{48,1},{49,0},{2,51}... | collective-permute-start | bytes 110600 | tf_op jit(solution)/shard_map/ppermute | solution.py:361
  31.4 1.6 %collective-permute-done.2.other = f32[9,8,128]{2,1,0:T(8,128)S(1)} collective-permute-done((f32[9,8,128]{2,1,0:T(8,128)S(1)}, f32[9,8,128]{2,1,0:T(8,128)S(1)}, u32[]{:S(2)}, u32[]{:S(2)}) %collective-permute-start.2) | collective-permute-done | bytes 36896 | tf_op jit(solution)/shard_map/ppermute | solution.py:361
  33.1 0.1 shard_map.91
  33.2 12.2 %all_to_all.11.got = f32[32,16,128]{2,1,0:T(8,128)S(1)} all-to-all(f32[32,16,128]{2,1,0:T(8,128)S(1)} %shard_map.91), channel_id=1, replica_groups=mesh['x'=4,'zh'=2,'z1'=2,'z0'=2,'y'=4,'sp'=2] {'x','z0','y'}, dimensions={0} | all-to-all | bytes 524288 | tf_op jit(solution)/shard_map/all_to_all | solution.py:367
  45.3 0.0 copy-done.1
  45.3 0.8 %shard_map.92 = (f32[2,256,128]{2,1,0:T(8,128)S(1)}, f32[2,256,128]{2,1,0:T(8,128)S(1)}) custom-call(f32[32,16,128]{2,1,0:T(8,128)S(1)} %all_to_all.11.got, f32[256,256]{1,0:T(8,128)S(1)} %get-tuple-element.27.rows_t, f32[128,128]{1,0:T(8,128)S(1)} %copy-done.1), custom_call_target="tpu_custom_call" | custom-call | tf_op jit(solution)/shard_map/pallas_call | solution.py:324
  46.1 0.2 collective-permute-start.3
  46.3 1.4 %collective-permute-done.3 = f32[2,256,128]{2,1,0:T(8,128)S(1)} collective-permute-done((f32[2,256,128]{2,1,0:T(8,128)S(1)}, f32[2,256,128]{2,1,0:T(8,128)S(1)}, u32[]{:S(2)}, u32[]{:S(2)}) %collective-permute-start.3) | collective-permute-done | bytes 262176 | tf_op jit(solution)/shard_map/ppermute | solution.py:371
  47.7 0.7 %slice_add_fusion = (f32[1,256,128]{2,1,0:T(8,128)}, f32[1,256,128]{2,1,0:T(8,128)}) fusion(f32[2,256,128]{2,1,0:T(8,128)S(1)} %collective-permute-done.3, f32[2,256,128]{2,1,0:T(8,128)S(1)} %get-tuple-element.28), kind=kLoop, calls=%fused_computation | loop fusion | flops 65536 | bytes 786432 | tf_op jit(solution)/shard_map/add | solution.py:372
  (1 shorter events, 0.0 us)
Async XLA Ops:
  0.6 4.6 %copy-start = (f32[128,128]{1,0:T(8,128)S(1)}, f32[128,128]{1,0:T(8,128)}, u32[]{:S(2)}) copy-start(f32[128,128]{1,0:T(8,128)} %constant.13.clone.col) | copy-start | bytes 196612
  0.6 44.7 %copy-start.1 = (f32[128,128]{1,0:T(8,128)S(1)}, f32[128,128]{1,0:T(8,128)}, u32[]{:S(2)}) copy-start(f32[128,128]{1,0:T(8,128)} %constant.14.clone.col) | copy-start | bytes 196612
  0.7 4.6 %collective-permute-start = (f32[256,128]{1,0:T(8,128)}, f32[256,128]{1,0:T(8,128)S(1)}, u32[]{:S(2)}, u32[]{:S(2)}) collective-permute-start(f32[256,128]{1,0:T(8,128)} %bitcast.3), channel_id=1, source_target_pairs={{0,1},{1,0},{2,3},{3,2},{4,5},{5,4},{6,7},{7,6},{8,9},{9,8},{10,11... | collective-permute-start | bytes 393224 | tf_op jit(solution)/shard_map/ppermute | solution.py:339
  20.3 6.6 %collective-permute-start.1 = (f32[2,4,8,128]{3,2,1,0:T(8,128)S(1)}, f32[2,4,8,128]{3,2,1,0:T(8,128)S(1)}, u32[]{:S(2)}, u32[]{:S(2)}) collective-permute-start(f32[2,4,8,128]{3,2,1,0:T(8,128)S(1)} %get-tuple-element.23.own), channel_id=1, source_target_pairs={{0,17},{1,16},{16,1},{17,0},{2,19},{3,18},{18,3},{19,2},{4,21},{5,... | collective-permute-start | bytes 98312 | tf_op jit(solution)/shard_map/ppermute | solution.py:356
  26.9 6.1 %collective-permute-start.2 = (f32[9,8,128]{2,1,0:T(8,128)S(1)}, f32[9,8,128]{2,1,0:T(8,128)S(1)}, u32[]{:S(2)}, u32[]{:S(2)}) collective-permute-start(f32[9,8,128]{2,1,0:T(8,128)S(1)} %get-tuple-element.26.own), channel_id=1, source_target_pairs={{0,49},{1,48},{16,33},{17,32},{32,17},{33,16},{48,1},{49,0},{2,51}... | collective-permute-start | bytes 110600 | tf_op jit(solution)/shard_map/ppermute | solution.py:361
  46.1 1.6 %collective-permute-start.3 = (f32[2,256,128]{2,1,0:T(8,128)S(1)}, f32[2,256,128]{2,1,0:T(8,128)S(1)}, u32[]{:S(2)}, u32[]{:S(2)}) collective-permute-start(f32[2,256,128]{2,1,0:T(8,128)S(1)} %get-tuple-element.29), channel_id=1, source_target_pairs={{0,1},{1,0},{2,3},{3,2},{4,5},{5,4},{6,7},{7,6},{8,9},{9,8},{10,11... | collective-permute-start | bytes 786440 | tf_op jit(solution)/shard_map/ppermute | solution.py:371

commit v2 on v1

--- a/solution.py
+++ b/solution.py
@@ -1,5 +1,6 @@
 import jax
 import jax.numpy as jnp
+import ml_dtypes
 import numpy as np
 from jax import lax
 from jax.experimental import pallas as pl
@@ -89,7 +90,7 @@
     turns = slice_rows()[..., None] * np.arange(HALF) % ROWS
     angle = 2 * np.pi * turns / ROWS
     table = np.concatenate([np.cos(angle), np.sin(angle)], axis=2)
-    return table.reshape(2, HALF, HALF).astype(np.float32)
+    return table.reshape(2, HALF, HALF)
 
 
 def column_tables():
@@ -99,22 +100,65 @@
     forward = np.concatenate([np.cos(angle), -np.sin(angle)], 1)
     forward[:, LANES] = np.where(np.arange(COLS) % 2 == 0, 1.0, -1.0)
     backward = 2.0 * forward.T / (ROWS * COLS)
-    return forward.astype(np.float32), backward.astype(np.float32)
+    return forward, backward
+
+
+def constant_terms(table, count):
+    found, rest = [], table.astype(np.float64)
+    for _ in range(count):
+        found.append(rest.astype(ml_dtypes.bfloat16))
+        rest = rest - found[-1].astype(np.float64)
+    return found
+
+
+def split_table(table, count):
+    return np.concatenate(constant_terms(table, count), axis=-1)
+
+
+def joined_table(table, pairs):
+    found = constant_terms(table, 1 + max(j for _, j in pairs))
+    return np.concatenate([found[j] for _, j in pairs], axis=0)
 
 
 def dot(a, b):
     return jnp.dot(a, b, precision=HIGHEST, preferred_element_type=jnp.float32)
 
 
-def halves(x):
-    high = x.astype(jnp.bfloat16)
-    return high, (x - high.astype(jnp.float32)).astype(jnp.bfloat16)
-
-
-def dot_split(a, b):
-    (ah, al), (bh, bl) = halves(a), halves(b)
-    one = lambda x, y: jnp.dot(x, y, preferred_element_type=jnp.float32)
-    return one(ah, bh) + (one(ah, bl) + one(al, bh))
+SIX = ((0, 0), (1, 0), (2, 0), (0, 1), (1, 1), (0, 2))
+THREE = ((0, 0), (1, 0), (0, 1))
+
+
+def terms(x, count):
+    found = []
+    for _ in range(count):
+        found.append(x.astype(jnp.bfloat16))
+        x = x - found[-1].astype(jnp.float32)
+    return found
+
+
+def joined(parts, order, axis):
+    return jnp.concatenate([parts[n] for n in order], axis=axis)
+
+
+def by_halves(left, right):
+    half = left.shape[0] // 2
+    rows = (left[:half], left[half:])
+    return jnp.concatenate(
+        [jnp.dot(part, right, preferred_element_type=jnp.float32) for part in rows], axis=0
+    )
+
+
+def times_table(x, table, pairs):
+    left = joined(terms(x, 1 + max(i for i, _ in pairs)), [i for i, _ in pairs], 1)
+    return by_halves(left, table)
+
+
+def table_times(table, x, pairs):
+    depth = x.shape[0]
+    parts = [table[:, n * depth : (n + 1) * depth] for n in range(table.shape[1] // depth)]
+    left = joined(parts, [j for _, j in pairs], 1)
+    right = joined(terms(x, 1 + max(i for i, _ in pairs)), [i for i, _ in pairs], 0)
+    return by_halves(left, right)
 
 
 def swap(x):
@@ -141,7 +185,9 @@
     return (lax.axis_index("sp") + lax.axis_index("z1")) % 2
 
 
-def prepare_kernel(src, init, rows, rows_t, table, src_o, init_o, rows_o, rows_t_o, table_o, sems):
+def prepare_kernel(
+    src, init, rows, rows_t, few, table, src_o, init_o, rows_o, rows_t_o, few_o, table_o, sems
+):
     kind = parity()
     pairs = (
         (src, src_o),
@@ -149,6 +195,7 @@
         (init, init_o),
         (table.at[kind, own_slice()], table_o),
         (rows_t.at[kind], rows_t_o),
+        (few.at[kind, own_slice()], few_o),
     )
     copies = [pltpu.make_async_copy(a, b, sems.at[n]) for n, (a, b) in enumerate(pairs)]
     for copy in copies:
@@ -183,20 +230,20 @@
 
 
 def columns(folded, col):
-    y = dot(folded, col[...])
+    y = times_table(folded, col[...], SIX)
     return jnp.concatenate([y, y * alternating(y.shape)], axis=1)
 
 
 def forward_kernel(src, src_other, col, rows, out):
     first = parity() == 0
-    out[...] = to_modes(dot(rows[...], columns(fold(src, src_other), col)), first)
+    product = table_times(rows[...], columns(fold(src, src_other), col), SIX)
+    out[...] = to_modes(product, first)
 
 
 def initial_kernel(init, col, rows, out):
     at = own_slice()
-    own_rows = rows[pl.ds(pl.multiple_of(8 * at, 8), 8), :]
     first = jnp.logical_and(parity() == 0, at == 0)
-    part = to_modes(dot(own_rows, columns(init[...], col)), first)
+    part = to_modes(dot(rows[...], columns(init[...], col)), first)
     odd, lower = parity() == 1, lax.axis_index("sp") == 1
     out[...] = jnp.where(jnp.logical_and(odd, lower), -1.0, 1.0) * part
 
@@ -299,7 +346,7 @@
     flat = lambda v: v.reshape(HALF, COLS)
     left = [flat(jnp.where(sub < QUAD, v, -v)) for v in parts]
     right = [flat(flip(v)) for v in parts]
-    product = dot_split(rows_t[...], jnp.concatenate(left + right, axis=1))
+    product = table_times(rows_t[...], jnp.concatenate(left + right, axis=1), THREE)
     sign = alternating((HALF, COLS))
     lane = iota((HALF, COLS), 1)
     own_sign = jnp.where(jnp.logical_and(odd, lower), -1.0, 1.0)
@@ -311,7 +358,8 @@
         y = jnp.where(lane < LANES, e + sign * swap(e), swap(f) + sign * f)
         first_u, first_v = v[0, :1], v[0, QUAD : QUAD + 1]
         edge = e + zero_mode * (sign * first_v - first_u)
-        part = dot_split(jnp.where(lane % LANES == 0, edge, y), col[...]) + constants[n]
+        y = jnp.where(lane % LANES == 0, edge, y)
+        part = times_table(y, col[...], THREE) + constants[n]
         out[n] = sent_sign * part
         own_out[n] = own_sign * part
 
@@ -323,7 +371,9 @@
     space = pltpu.HBM if hbm else pltpu.VMEM
     return pl.pallas_call(
         kernel,
-        out_shape=[jax.ShapeDtypeStruct(s, jnp.float32) for s in shapes],
+        out_shape=[
+            jax.ShapeDtypeStruct(s, jnp.float32) if isinstance(s, tuple) else s for s in shapes
+        ],
         in_specs=[pl.BlockSpec(memory_space=space)] * len(args),
         out_specs=[pl.BlockSpec(memory_space=pltpu.VMEM)] * len(shapes),
         scratch_shapes=scratch,
@@ -334,19 +384,30 @@
 def shards(initial, source):
     rows = row_table()
     forward, backward = column_tables()
+    forward, backward = joined_table(forward, SIX), joined_table(backward, THREE)
+    rows_split = split_table(rows, 3)
+    rows_t_split = split_table(rows.transpose(0, 2, 1), 2)
+    few_rows = rows.reshape(2, GROUP, 8, HALF).astype(np.float32)
     own = source[0]
     swap_two = [(0, 1), (1, 0)]
     src_other = lax.ppermute(own, "sp", swap_two)
     block = (HALF, COLS)
-    square = (HALF, HALF)
-    constants = [rows, rows.transpose(0, 2, 1).copy(), mode_table()]
+    constants = [rows_split, rows_t_split, few_rows, mode_table()]
     args = [own, initial, *(jnp.asarray(a) for a in constants)]
-    src, init, rows_v, rows_t_v, table = call(
+    bf16 = jnp.bfloat16
+    src, init, rows_v, rows_t_v, few, table = call(
         prepare_kernel,
-        [block, block, square, square, (16 * N_OPS, COLS)],
+        [
+            block,
+            block,
+            jax.ShapeDtypeStruct((HALF, 3 * HALF), bf16),
+            jax.ShapeDtypeStruct((HALF, 2 * HALF), bf16),
+            (8, HALF),
+            (16 * N_OPS, COLS),
+        ],
         [pltpu.with_memory_space_constraint(a, pltpu.HBM) for a in args],
         hbm=True,
-        scratch=[pltpu.SemaphoreType.DMA((5,))],
+        scratch=[pltpu.SemaphoreType.DMA((6,))],
     )
     (sent,) = call(forward_kernel, [block], [src, src_other, forward, rows_v])
     got = lax.all_to_all(sent.reshape(GROUP, 8, COLS), PLANE, 0, 0, tiled=True)
@@ -354,7 +415,7 @@
     c, mean, message = call(scan_kernel, [runs, runs, ends], [got, table])
     init, message = lax.optimization_barrier((init, message))
     other = lax.ppermute(message, ("z1", "sp"), [(i, i ^ 3) for i in range(4)])
-    (init_part,) = call(initial_kernel, [(8, COLS)], [init, forward, rows_v])
+    (init_part,) = call(initial_kernel, [(8, COLS)], [init, forward, few])
     message, kept = call(
         join_kernel, [(9, 8, COLS), ends], [message, other, init_part, table]
     )

time: 48.6 us -> 48.5 us (level)
  no operation moved by 1% of the time
where the time goes in v2:
time: 48.5 us; the launch traced here: 48.3 us
  blocking collectives  26.2 us (54%)
  starting transfers between devices  12.7 us (26%)
  waiting for transfers between devices  4.4 us (9%)
  Pallas kernels  3.53 us (7%)
  other arithmetic  0.74 us (2%)
  between operations  0.7 us (1%)
    all_to_all x1, blocking collectives, shards(): got = lax.all_to_all(sent.reshape(GROUP, 8, COLS), PLANE, 0, 0, tiled=True)  14 us
    all_to_all x1, blocking collectives, shards(): modes = lax.all_to_all(back, PLANE, 0, 0, tiled=True)  12.2 us
    ppermute x1, starting transfers between devices, shards(): other = lax.ppermute(message, ('z1', 'sp'), [(i, i ^ 3) for i in range(4)])  4.64 us
    ppermute x1, starting transfers between devices, shards(): lax.ppermute(message, ('zh', 'z1', 'sp'), [(i, i ^ 7) for i in range(8)])  4.5 us
    pallas_call x7, Pallas kernels, call(): pl.pallas_call(kernel, out_shape=[jax.ShapeDtypeStruct(s, jnp.float32) if...  3.53 us
    ppermute x1, starting transfers between devices, shards(): src_other = lax.ppermute(own, 'sp', swap_two)  3.33 us
    ppermute x1, waiting for transfers between devices, shards(): lax.ppermute(message, ('zh', 'z1', 'sp'), [(i, i ^ 7) for i in range(8)])  1.64 us
    ppermute x1, waiting for transfers between devices, shards(): other_part = lax.ppermute(part, 'sp', swap_two)  1.43 us
  transfers between devices with their start and end apart: 4, of which 3 were waited for; matrix products, arithmetic and copies ran while one was open for 0% of the time, Pallas kernels for 4%

profile of v2, /device:TPU:1, one launch (start us, length us, event | category | flops | bytes accessed | tf_op | source)
XLA Modules:
  0.0 48.3 jit_solution(12564656824783679859)
XLA Ops:
  0.6 0.0 copy-start
  0.6 0.0 copy-start.1
  0.7 3.3 %collective-permute-start = (f32[256,128]{1,0:T(8,128)}, f32[256,128]{1,0:T(8,128)S(1)}, u32[]{:S(2)}, u32[]{:S(2)}) collective-permute-start(f32[256,128]{1,0:T(8,128)} %bitcast.3), channel_id=1, source_target_pairs={{0,1},{1,0},{2,3},{3,2},{4,5},{5,4},{6,7},{7,6},{8,9},{9,8},{10,11... | collective-permute-start | bytes 393224 | tf_op jit(solution)/shard_map/ppermute | solution.py:393
  4.0 1.3 %shard_map.95 = (f32[256,128]{1,0:T(8,128)S(1)}, f32[256,128]{1,0:T(8,128)S(1)}, bf16[256,768]{1,0:T(8,128)(2,1)S(1)}, bf16[256,512]{1,0:T(8,128)(2,1)S(1)}, f32...) custom-call(f32[256,128]{1,0:T(8,128)} %bitcast.4, f32[256,128]{1,0:T(8,128)} %init.1, ...), custom_call_target="tpu_custom_call" | custom-call | tf_op jit(solution)/shard_map/pallas_call | solution.py:372
  5.3 0.0 collective-permute-done.src_other
  5.3 0.0 copy-done
  5.3 0.7 %shard_map.96 = f32[256,128]{1,0:T(8,128)S(1)} custom-call(f32[256,128]{1,0:T(8,128)S(1)} %get-tuple-element.17.src, f32[256,128]{1,0:T(8,128)S(1)} %collective-permute-done.src_other, bf16[768,128]{1,0:T(8,128)(2,1)S(1)} %copy-done, bf16[256,768]{1,0:T(8,128)(2,1)S(1)} %get-tuple-element.18.rows), custom_call_target="tpu_custom_call" | custom-call | tf_op jit(solution)/shard_map/pallas_call | solution.py:372
  6.0 14.0 %all_to_all.10.got = f32[32,8,128]{2,1,0:T(8,128)S(1)} all-to-all(f32[32,8,128]{2,1,0:T(8,128)S(1)} %bitcast.2), channel_id=1, replica_groups=mesh['x'=4,'zh'=2,'z1'=2,'z0'=2,'y'=4,'sp'=2] {'x','z0','y'}, dimensions={0} | all-to-all | bytes 262144 | tf_op jit(solution)/shard_map/all_to_all | solution.py:413
  20.0 0.1 shard_map.97
  20.2 4.6 %collective-permute-start.1 = (f32[2,4,8,128]{3,2,1,0:T(8,128)S(1)}, f32[2,4,8,128]{3,2,1,0:T(8,128)S(1)}, u32[]{:S(2)}, u32[]{:S(2)}) collective-permute-start(f32[2,4,8,128]{3,2,1,0:T(8,128)S(1)} %get-tuple-element.24.own), channel_id=1, source_target_pairs={{0,17},{1,16},{16,1},{17,0},{2,19},{3,18},{18,3},{19,2},{4,21},{5,... | collective-permute-start | bytes 98312 | tf_op jit(solution)/shard_map/ppermute | solution.py:417
  24.8 0.6 %shard_map.98.init = f32[8,128]{1,0:T(8,128)S(1)} custom-call(f32[256,128]{1,0:T(8,128)S(1)} %get-tuple-element.25.init, bf16[768,128]{1,0:T(8,128)(2,1)S(1)} %copy-done, f32[8,256]{1,0:T(8,128)S(1)} %get-tuple-element.26.rows), custom_call_target="tpu_custom_call" | custom-call | tf_op jit(solution)/shard_map/pallas_call | solution.py:372
  25.4 1.3 %collective-permute-done.1.other = f32[2,4,8,128]{3,2,1,0:T(8,128)S(1)} collective-permute-done((f32[2,4,8,128]{3,2,1,0:T(8,128)S(1)}, f32[2,4,8,128]{3,2,1,0:T(8,128)S(1)}, u32[]{:S(2)}, u32[]{:S(2)}) %collective-permute-start.1) | collective-permute-done | bytes 32800 | tf_op jit(solution)/shard_map/ppermute | solution.py:417
  26.8 4.5 %collective-permute-start.2 = (f32[9,8,128]{2,1,0:T(8,128)S(1)}, f32[9,8,128]{2,1,0:T(8,128)S(1)}, u32[]{:S(2)}, u32[]{:S(2)}) collective-permute-start(f32[9,8,128]{2,1,0:T(8,128)S(1)} %get-tuple-element.28.own), channel_id=1, source_target_pairs={{0,49},{1,48},{16,33},{17,32},{32,17},{33,16},{48,1},{49,0},{2,51}... | collective-permute-start | bytes 110600 | tf_op jit(solution)/shard_map/ppermute | solution.py:422
  31.3 1.6 %collective-permute-done.2.other = f32[9,8,128]{2,1,0:T(8,128)S(1)} collective-permute-done((f32[9,8,128]{2,1,0:T(8,128)S(1)}, f32[9,8,128]{2,1,0:T(8,128)S(1)}, u32[]{:S(2)}, u32[]{:S(2)}) %collective-permute-start.2) | collective-permute-done | bytes 36896 | tf_op jit(solution)/shard_map/ppermute | solution.py:422
  32.9 0.1 shard_map.100
  33.0 12.2 %all_to_all.11.got = f32[32,16,128]{2,1,0:T(8,128)S(1)} all-to-all(f32[32,16,128]{2,1,0:T(8,128)S(1)} %shard_map.100), channel_id=1, replica_groups=mesh['x'=4,'zh'=2,'z1'=2,'z0'=2,'y'=4,'sp'=2] {'x','z0','y'}, dimensions={0} | all-to-all | bytes 524288 | tf_op jit(solution)/shard_map/all_to_all | solution.py:428
  45.2 0.0 copy-done.1
  45.2 0.7 %shard_map.101 = (f32[2,256,128]{2,1,0:T(8,128)S(1)}, f32[2,256,128]{2,1,0:T(8,128)S(1)}) custom-call(f32[32,16,128]{2,1,0:T(8,128)S(1)} %all_to_all.11.got, bf16[256,512]{1,0:T(8,128)(2,1)S(1)} %get-tuple-element.29.rows_t, bf16[384,128]{1,0:T(8,128)(2,1)S(1)} %copy-done.1), custom_call_target="tpu_custom_call" | custom-call | tf_op jit(solution)/shard_map/pallas_call | solution.py:372
  45.9 0.2 collective-permute-start.3
  46.1 1.4 %collective-permute-done.3 = f32[2,256,128]{2,1,0:T(8,128)S(1)} collective-permute-done((f32[2,256,128]{2,1,0:T(8,128)S(1)}, f32[2,256,128]{2,1,0:T(8,128)S(1)}, u32[]{:S(2)}, u32[]{:S(2)}) %collective-permute-start.3) | collective-permute-done | bytes 262176 | tf_op jit(solution)/shard_map/ppermute | solution.py:432
  47.5 0.7 %slice_add_fusion = (f32[1,256,128]{2,1,0:T(8,128)}, f32[1,256,128]{2,1,0:T(8,128)}) fusion(f32[2,256,128]{2,1,0:T(8,128)S(1)} %collective-permute-done.3, f32[2,256,128]{2,1,0:T(8,128)S(1)} %get-tuple-element.30), kind=kLoop, calls=%fused_computation | loop fusion | flops 65536 | bytes 786432 | tf_op jit(solution)/shard_map/add | solution.py:433
  (1 shorter events, 0.0 us)
Async XLA Ops:
  0.6 4.6 %copy-start = (bf16[768,128]{1,0:T(8,128)(2,1)S(1)}, bf16[768,128]{1,0:T(8,128)(2,1)}, u32[]{:S(2)}) copy-start(bf16[768,128]{1,0:T(8,128)(2,1)} %constant.16.clone.col) | copy-start | bytes 589828
  0.6 44.6 %copy-start.1 = (bf16[384,128]{1,0:T(8,128)(2,1)S(1)}, bf16[384,128]{1,0:T(8,128)(2,1)}, u32[]{:S(2)}) copy-start(bf16[384,128]{1,0:T(8,128)(2,1)} %constant.17.clone.col) | copy-start | bytes 294916
  0.7 4.6 %collective-permute-start = (f32[256,128]{1,0:T(8,128)}, f32[256,128]{1,0:T(8,128)S(1)}, u32[]{:S(2)}, u32[]{:S(2)}) collective-permute-start(f32[256,128]{1,0:T(8,128)} %bitcast.3), channel_id=1, source_target_pairs={{0,1},{1,0},{2,3},{3,2},{4,5},{5,4},{6,7},{7,6},{8,9},{9,8},{10,11... | collective-permute-start | bytes 393224 | tf_op jit(solution)/shard_map/ppermute | solution.py:393
  20.2 6.6 %collective-permute-start.1 = (f32[2,4,8,128]{3,2,1,0:T(8,128)S(1)}, f32[2,4,8,128]{3,2,1,0:T(8,128)S(1)}, u32[]{:S(2)}, u32[]{:S(2)}) collective-permute-start(f32[2,4,8,128]{3,2,1,0:T(8,128)S(1)} %get-tuple-element.24.own), channel_id=1, source_target_pairs={{0,17},{1,16},{16,1},{17,0},{2,19},{3,18},{18,3},{19,2},{4,21},{5,... | collective-permute-start | bytes 98312 | tf_op jit(solution)/shard_map/ppermute | solution.py:417
  26.8 6.1 %collective-permute-start.2 = (f32[9,8,128]{2,1,0:T(8,128)S(1)}, f32[9,8,128]{2,1,0:T(8,128)S(1)}, u32[]{:S(2)}, u32[]{:S(2)}) collective-permute-start(f32[9,8,128]{2,1,0:T(8,128)S(1)} %get-tuple-element.28.own), channel_id=1, source_target_pairs={{0,49},{1,48},{16,33},{17,32},{32,17},{33,16},{48,1},{49,0},{2,51}... | collective-permute-start | bytes 110600 | tf_op jit(solution)/shard_map/ppermute | solution.py:422
  45.9 1.6 %collective-permute-start.3 = (f32[2,256,128]{2,1,0:T(8,128)S(1)}, f32[2,256,128]{2,1,0:T(8,128)S(1)}, u32[]{:S(2)}, u32[]{:S(2)}) collective-permute-start(f32[2,256,128]{2,1,0:T(8,128)S(1)} %get-tuple-element.31), channel_id=1, source_target_pairs={{0,1},{1,0},{2,3},{3,2},{4,5},{5,4},{6,7},{7,6},{8,9},{9,8},{10,11... | collective-permute-start | bytes 786440 | tf_op jit(solution)/shard_map/ppermute | solution.py:432

commit v3 on v2

--- a/solution.py
+++ b/solution.py
@@ -158,7 +158,11 @@
     parts = [table[:, n * depth : (n + 1) * depth] for n in range(table.shape[1] // depth)]
     left = joined(parts, [j for _, j in pairs], 1)
     right = joined(terms(x, 1 + max(i for i, _ in pairs)), [i for i, _ in pairs], 0)
-    return by_halves(left, right)
+    if len(pairs) % 2:
+        return by_halves(left, right)
+    cut = left.shape[1] // 2
+    near = jnp.dot(left[:, :cut], right[:cut], preferred_element_type=jnp.float32)
+    return near + jnp.dot(left[:, cut:], right[cut:], preferred_element_type=jnp.float32)
 
 
 def swap(x):

time: 48.5 us -> 48.4 us (level)
  no operation moved by 1% of the time
where the time goes in v3:
time: 48.4 us; the launch traced here: 48.2 us
  blocking collectives  26.2 us (54%)
  starting transfers between devices  12.7 us (26%)
  waiting for transfers between devices  4.4 us (9%)
  Pallas kernels  3.5 us (7%)
  other arithmetic  0.74 us (2%)
  between operations  0.69 us (1%)
    all_to_all x1, blocking collectives, shards(): got = lax.all_to_all(sent.reshape(GROUP, 8, COLS), PLANE, 0, 0, tiled=True)  14 us
    all_to_all x1, blocking collectives, shards(): modes = lax.all_to_all(back, PLANE, 0, 0, tiled=True)  12.2 us
    ppermute x1, starting transfers between devices, shards(): other = lax.ppermute(message, ('z1', 'sp'), [(i, i ^ 3) for i in range(4)])  4.64 us
    ppermute x1, starting transfers between devices, shards(): lax.ppermute(message, ('zh', 'z1', 'sp'), [(i, i ^ 7) for i in range(8)])  4.5 us
    pallas_call x7, Pallas kernels, call(): pl.pallas_call(kernel, out_shape=[jax.ShapeDtypeStruct(s, jnp.float32) if...  3.5 us
    ppermute x1, starting transfers between devices, shards(): src_other = lax.ppermute(own, 'sp', swap_two)  3.33 us
    ppermute x1, waiting for transfers between devices, shards(): lax.ppermute(message, ('zh', 'z1', 'sp'), [(i, i ^ 7) for i in range(8)])  1.64 us
    ppermute x1, waiting for transfers between devices, shards(): other_part = lax.ppermute(part, 'sp', swap_two)  1.43 us
  transfers between devices with their start and end apart: 4, of which 3 were waited for; matrix products, arithmetic and copies ran while one was open for 0% of the time, Pallas kernels for 4%

profile of v3, /device:TPU:1, one launch (start us, length us, event | category | flops | bytes accessed | tf_op | source)
XLA Modules:
  0.0 48.2 jit_solution(1480319379254553828)
XLA Ops:
  0.6 0.0 copy-start
  0.6 0.0 copy-start.1
  0.7 3.3 %collective-permute-start = (f32[256,128]{1,0:T(8,128)}, f32[256,128]{1,0:T(8,128)S(1)}, u32[]{:S(2)}, u32[]{:S(2)}) collective-permute-start(f32[256,128]{1,0:T(8,128)} %bitcast.3), channel_id=1, source_target_pairs={{0,1},{1,0},{2,3},{3,2},{4,5},{5,4},{6,7},{7,6},{8,9},{9,8},{10,11... | collective-permute-start | bytes 393224 | tf_op jit(solution)/shard_map/ppermute | solution.py:397
  4.0 1.3 %shard_map.95 = (f32[256,128]{1,0:T(8,128)S(1)}, f32[256,128]{1,0:T(8,128)S(1)}, bf16[256,768]{1,0:T(8,128)(2,1)S(1)}, bf16[256,512]{1,0:T(8,128)(2,1)S(1)}, f32...) custom-call(f32[256,128]{1,0:T(8,128)} %bitcast.4, f32[256,128]{1,0:T(8,128)} %init.1, ...), custom_call_target="tpu_custom_call" | custom-call | tf_op jit(solution)/shard_map/pallas_call | solution.py:376
  5.3 0.0 collective-permute-done.src_other
  5.3 0.0 copy-done
  5.3 0.7 %shard_map.96 = f32[256,128]{1,0:T(8,128)S(1)} custom-call(f32[256,128]{1,0:T(8,128)S(1)} %get-tuple-element.17.src, f32[256,128]{1,0:T(8,128)S(1)} %collective-permute-done.src_other, bf16[768,128]{1,0:T(8,128)(2,1)S(1)} %copy-done, bf16[256,768]{1,0:T(8,128)(2,1)S(1)} %get-tuple-element.18.rows), custom_call_target="tpu_custom_call" | custom-call | tf_op jit(solution)/shard_map/pallas_call | solution.py:376
  6.0 14.0 %all_to_all.10.got = f32[32,8,128]{2,1,0:T(8,128)S(1)} all-to-all(f32[32,8,128]{2,1,0:T(8,128)S(1)} %bitcast.2), channel_id=1, replica_groups=mesh['x'=4,'zh'=2,'z1'=2,'z0'=2,'y'=4,'sp'=2] {'x','z0','y'}, dimensions={0} | all-to-all | bytes 262144 | tf_op jit(solution)/shard_map/all_to_all | solution.py:417
  20.0 0.1 shard_map.97
  20.1 4.6 %collective-permute-start.1 = (f32[2,4,8,128]{3,2,1,0:T(8,128)S(1)}, f32[2,4,8,128]{3,2,1,0:T(8,128)S(1)}, u32[]{:S(2)}, u32[]{:S(2)}) collective-permute-start(f32[2,4,8,128]{3,2,1,0:T(8,128)S(1)} %get-tuple-element.24.own), channel_id=1, source_target_pairs={{0,17},{1,16},{16,1},{17,0},{2,19},{3,18},{18,3},{19,2},{4,21},{5,... | collective-permute-start | bytes 98312 | tf_op jit(solution)/shard_map/ppermute | solution.py:421
  24.8 0.6 %shard_map.98.init = f32[8,128]{1,0:T(8,128)S(1)} custom-call(f32[256,128]{1,0:T(8,128)S(1)} %get-tuple-element.25.init, bf16[768,128]{1,0:T(8,128)(2,1)S(1)} %copy-done, f32[8,256]{1,0:T(8,128)S(1)} %get-tuple-element.26.rows), custom_call_target="tpu_custom_call" | custom-call | tf_op jit(solution)/shard_map/pallas_call | solution.py:376
  25.4 1.3 %collective-permute-done.1.other = f32[2,4,8,128]{3,2,1,0:T(8,128)S(1)} collective-permute-done((f32[2,4,8,128]{3,2,1,0:T(8,128)S(1)}, f32[2,4,8,128]{3,2,1,0:T(8,128)S(1)}, u32[]{:S(2)}, u32[]{:S(2)}) %collective-permute-start.1) | collective-permute-done | bytes 32800 | tf_op jit(solution)/shard_map/ppermute | solution.py:421
  26.7 4.5 %collective-permute-start.2 = (f32[9,8,128]{2,1,0:T(8,128)S(1)}, f32[9,8,128]{2,1,0:T(8,128)S(1)}, u32[]{:S(2)}, u32[]{:S(2)}) collective-permute-start(f32[9,8,128]{2,1,0:T(8,128)S(1)} %get-tuple-element.28.own), channel_id=1, source_target_pairs={{0,49},{1,48},{16,33},{17,32},{32,17},{33,16},{48,1},{49,0},{2,51}... | collective-permute-start | bytes 110600 | tf_op jit(solution)/shard_map/ppermute | solution.py:426
  31.2 1.6 %collective-permute-done.2.other = f32[9,8,128]{2,1,0:T(8,128)S(1)} collective-permute-done((f32[9,8,128]{2,1,0:T(8,128)S(1)}, f32[9,8,128]{2,1,0:T(8,128)S(1)}, u32[]{:S(2)}, u32[]{:S(2)}) %collective-permute-start.2) | collective-permute-done | bytes 36896 | tf_op jit(solution)/shard_map/ppermute | solution.py:426
  32.9 0.1 shard_map.100
  33.0 12.2 %all_to_all.11.got = f32[32,16,128]{2,1,0:T(8,128)S(1)} all-to-all(f32[32,16,128]{2,1,0:T(8,128)S(1)} %shard_map.100), channel_id=1, replica_groups=mesh['x'=4,'zh'=2,'z1'=2,'z0'=2,'y'=4,'sp'=2] {'x','z0','y'}, dimensions={0} | all-to-all | bytes 524288 | tf_op jit(solution)/shard_map/all_to_all | solution.py:432
  45.2 0.0 copy-done.1
  45.2 0.7 %shard_map.101 = (f32[2,256,128]{2,1,0:T(8,128)S(1)}, f32[2,256,128]{2,1,0:T(8,128)S(1)}) custom-call(f32[32,16,128]{2,1,0:T(8,128)S(1)} %all_to_all.11.got, bf16[256,512]{1,0:T(8,128)(2,1)S(1)} %get-tuple-element.29.rows_t, bf16[384,128]{1,0:T(8,128)(2,1)S(1)} %copy-done.1), custom_call_target="tpu_custom_call" | custom-call | tf_op jit(solution)/shard_map/pallas_call | solution.py:376
  45.9 0.2 collective-permute-start.3
  46.1 1.4 %collective-permute-done.3 = f32[2,256,128]{2,1,0:T(8,128)S(1)} collective-permute-done((f32[2,256,128]{2,1,0:T(8,128)S(1)}, f32[2,256,128]{2,1,0:T(8,128)S(1)}, u32[]{:S(2)}, u32[]{:S(2)}) %collective-permute-start.3) | collective-permute-done | bytes 262176 | tf_op jit(solution)/shard_map/ppermute | solution.py:436
  47.5 0.7 %slice_add_fusion = (f32[1,256,128]{2,1,0:T(8,128)}, f32[1,256,128]{2,1,0:T(8,128)}) fusion(f32[2,256,128]{2,1,0:T(8,128)S(1)} %collective-permute-done.3, f32[2,256,128]{2,1,0:T(8,128)S(1)} %get-tuple-element.30), kind=kLoop, calls=%fused_computation | loop fusion | flops 65536 | bytes 786432 | tf_op jit(solution)/shard_map/add | solution.py:437
  (1 shorter events, 0.0 us)
Async XLA Ops:
  0.6 4.6 %copy-start = (bf16[768,128]{1,0:T(8,128)(2,1)S(1)}, bf16[768,128]{1,0:T(8,128)(2,1)}, u32[]{:S(2)}) copy-start(bf16[768,128]{1,0:T(8,128)(2,1)} %constant.16.clone.col) | copy-start | bytes 589828
  0.6 44.5 %copy-start.1 = (bf16[384,128]{1,0:T(8,128)(2,1)S(1)}, bf16[384,128]{1,0:T(8,128)(2,1)}, u32[]{:S(2)}) copy-start(bf16[384,128]{1,0:T(8,128)(2,1)} %constant.17.clone.col) | copy-start | bytes 294916
  0.7 4.6 %collective-permute-start = (f32[256,128]{1,0:T(8,128)}, f32[256,128]{1,0:T(8,128)S(1)}, u32[]{:S(2)}, u32[]{:S(2)}) collective-permute-start(f32[256,128]{1,0:T(8,128)} %bitcast.3), channel_id=1, source_target_pairs={{0,1},{1,0},{2,3},{3,2},{4,5},{5,4},{6,7},{7,6},{8,9},{9,8},{10,11... | collective-permute-start | bytes 393224 | tf_op jit(solution)/shard_map/ppermute | solution.py:397
  20.1 6.6 %collective-permute-start.1 = (f32[2,4,8,128]{3,2,1,0:T(8,128)S(1)}, f32[2,4,8,128]{3,2,1,0:T(8,128)S(1)}, u32[]{:S(2)}, u32[]{:S(2)}) collective-permute-start(f32[2,4,8,128]{3,2,1,0:T(8,128)S(1)} %get-tuple-element.24.own), channel_id=1, source_target_pairs={{0,17},{1,16},{16,1},{17,0},{2,19},{3,18},{18,3},{19,2},{4,21},{5,... | collective-permute-start | bytes 98312 | tf_op jit(solution)/shard_map/ppermute | solution.py:421
  26.7 6.1 %collective-permute-start.2 = (f32[9,8,128]{2,1,0:T(8,128)S(1)}, f32[9,8,128]{2,1,0:T(8,128)S(1)}, u32[]{:S(2)}, u32[]{:S(2)}) collective-permute-start(f32[9,8,128]{2,1,0:T(8,128)S(1)} %get-tuple-element.28.own), channel_id=1, source_target_pairs={{0,49},{1,48},{16,33},{17,32},{32,17},{33,16},{48,1},{49,0},{2,51}... | collective-permute-start | bytes 110600 | tf_op jit(solution)/shard_map/ppermute | solution.py:426
  45.9 1.6 %collective-permute-start.3 = (f32[2,256,128]{2,1,0:T(8,128)S(1)}, f32[2,256,128]{2,1,0:T(8,128)S(1)}, u32[]{:S(2)}, u32[]{:S(2)}) collective-permute-start(f32[2,256,128]{2,1,0:T(8,128)S(1)} %get-tuple-element.31), channel_id=1, source_target_pairs={{0,1},{1,0},{2,3},{3,2},{4,5},{5,4},{6,7},{7,6},{8,9},{9,8},{10,11... | collective-permute-start | bytes 786440 | tf_op jit(solution)/shard_map/ppermute | solution.py:436

commit v4 on v3

--- a/solution.py
+++ b/solution.py
@@ -150,7 +150,11 @@
 
 def times_table(x, table, pairs):
     left = joined(terms(x, 1 + max(i for i, _ in pairs)), [i for i, _ in pairs], 1)
-    return by_halves(left, table)
+    if len(pairs) % 2:
+        return by_halves(left, table)
+    cut = 2 * left.shape[1] // 3
+    near = jnp.dot(left[:, :cut], table[:cut], preferred_element_type=jnp.float32)
+    return near + jnp.dot(left[:, cut:], table[cut:], preferred_element_type=jnp.float32)
 
 
 def table_times(table, x, pairs):

time: 48.4 us -> 48.5 us (level)
  no operation moved by 1% of the time
where the time goes in v4:
time: 48.5 us; the launch traced here: 48.4 us
  blocking collectives  26.2 us (54%)
  starting transfers between devices  12.7 us (26%)
  waiting for transfers between devices  4.34 us (9%)
  Pallas kernels  3.67 us (8%)
  other arithmetic  0.74 us (2%)
  between operations  0.7 us (1%)
    all_to_all x1, blocking collectives, shards(): got = lax.all_to_all(sent.reshape(GROUP, 8, COLS), PLANE, 0, 0, tiled=True)  14 us
    all_to_all x1, blocking collectives, shards(): modes = lax.all_to_all(back, PLANE, 0, 0, tiled=True)  12.2 us
    ppermute x1, starting transfers between devices, shards(): other = lax.ppermute(message, ('z1', 'sp'), [(i, i ^ 3) for i in range(4)])  4.64 us
    ppermute x1, starting transfers between devices, shards(): lax.ppermute(message, ('zh', 'z1', 'sp'), [(i, i ^ 7) for i in range(8)])  4.51 us
    pallas_call x7, Pallas kernels, call(): pl.pallas_call(kernel, out_shape=[jax.ShapeDtypeStruct(s, jnp.float32) if...  3.67 us
    ppermute x1, starting transfers between devices, shards(): src_other = lax.ppermute(own, 'sp', swap_two)  3.33 us
    ppermute x1, waiting for transfers between devices, shards(): lax.ppermute(message, ('zh', 'z1', 'sp'), [(i, i ^ 7) for i in range(8)])  1.64 us
    ppermute x1, waiting for transfers between devices, shards(): other_part = lax.ppermute(part, 'sp', swap_two)  1.43 us
  transfers between devices with their start and end apart: 4, of which 3 were waited for; matrix products, arithmetic and copies ran while one was open for 0% of the time, Pallas kernels for 4%

profile of v4, /device:TPU:1, one launch (start us, length us, event | category | flops | bytes accessed | tf_op | source)
XLA Modules:
  0.0 48.4 jit_solution(15549189607842379883)
XLA Ops:
  0.6 0.0 copy-start
  0.6 0.0 copy-start.1
  0.7 3.3 %collective-permute-start = (f32[256,128]{1,0:T(8,128)}, f32[256,128]{1,0:T(8,128)S(1)}, u32[]{:S(2)}, u32[]{:S(2)}) collective-permute-start(f32[256,128]{1,0:T(8,128)} %bitcast.3), channel_id=1, source_target_pairs={{0,1},{1,0},{2,3},{3,2},{4,5},{5,4},{6,7},{7,6},{8,9},{9,8},{10,11... | collective-permute-start | bytes 393224 | tf_op jit(solution)/shard_map/ppermute | solution.py:401
  4.0 1.3 %shard_map.95 = (f32[256,128]{1,0:T(8,128)S(1)}, f32[256,128]{1,0:T(8,128)S(1)}, bf16[256,768]{1,0:T(8,128)(2,1)S(1)}, bf16[256,512]{1,0:T(8,128)(2,1)S(1)}, f32...) custom-call(f32[256,128]{1,0:T(8,128)} %bitcast.4, f32[256,128]{1,0:T(8,128)} %init.1, ...), custom_call_target="tpu_custom_call" | custom-call | tf_op jit(solution)/shard_map/pallas_call | solution.py:380
  5.3 0.0 collective-permute-done.src_other
  5.3 0.0 copy-done
  5.3 0.8 %shard_map.96 = f32[256,128]{1,0:T(8,128)S(1)} custom-call(f32[256,128]{1,0:T(8,128)S(1)} %get-tuple-element.17.src, f32[256,128]{1,0:T(8,128)S(1)} %collective-permute-done.src_other, bf16[768,128]{1,0:T(8,128)(2,1)S(1)} %copy-done, bf16[256,768]{1,0:T(8,128)(2,1)S(1)} %get-tuple-element.18.rows), custom_call_target="tpu_custom_call" | custom-call | tf_op jit(solution)/shard_map/pallas_call | solution.py:380
  6.1 14.0 %all_to_all.10.got = f32[32,8,128]{2,1,0:T(8,128)S(1)} all-to-all(f32[32,8,128]{2,1,0:T(8,128)S(1)} %bitcast.2), channel_id=1, replica_groups=mesh['x'=4,'zh'=2,'z1'=2,'z0'=2,'y'=4,'sp'=2] {'x','z0','y'}, dimensions={0} | all-to-all | bytes 262144 | tf_op jit(solution)/shard_map/all_to_all | solution.py:421
  20.1 0.1 shard_map.97
  20.2 4.6 %collective-permute-start.1 = (f32[2,4,8,128]{3,2,1,0:T(8,128)S(1)}, f32[2,4,8,128]{3,2,1,0:T(8,128)S(1)}, u32[]{:S(2)}, u32[]{:S(2)}) collective-permute-start(f32[2,4,8,128]{3,2,1,0:T(8,128)S(1)} %get-tuple-element.24.own), channel_id=1, source_target_pairs={{0,17},{1,16},{16,1},{17,0},{2,19},{3,18},{18,3},{19,2},{4,21},{5,... | collective-permute-start | bytes 98312 | tf_op jit(solution)/shard_map/ppermute | solution.py:425
  24.9 0.7 %shard_map.98.init = f32[8,128]{1,0:T(8,128)S(1)} custom-call(f32[256,128]{1,0:T(8,128)S(1)} %get-tuple-element.25.init, bf16[768,128]{1,0:T(8,128)(2,1)S(1)} %copy-done, f32[8,256]{1,0:T(8,128)S(1)} %get-tuple-element.26.rows), custom_call_target="tpu_custom_call" | custom-call | tf_op jit(solution)/shard_map/pallas_call | solution.py:380
  25.6 1.3 %collective-permute-done.1.other = f32[2,4,8,128]{3,2,1,0:T(8,128)S(1)} collective-permute-done((f32[2,4,8,128]{3,2,1,0:T(8,128)S(1)}, f32[2,4,8,128]{3,2,1,0:T(8,128)S(1)}, u32[]{:S(2)}, u32[]{:S(2)}) %collective-permute-start.1) | collective-permute-done | bytes 32800 | tf_op jit(solution)/shard_map/ppermute | solution.py:425
  26.9 4.5 %collective-permute-start.2 = (f32[9,8,128]{2,1,0:T(8,128)S(1)}, f32[9,8,128]{2,1,0:T(8,128)S(1)}, u32[]{:S(2)}, u32[]{:S(2)}) collective-permute-start(f32[9,8,128]{2,1,0:T(8,128)S(1)} %get-tuple-element.28.own), channel_id=1, source_target_pairs={{0,49},{1,48},{16,33},{17,32},{32,17},{33,16},{48,1},{49,0},{2,51}... | collective-permute-start | bytes 110600 | tf_op jit(solution)/shard_map/ppermute | solution.py:430
  31.4 1.6 %collective-permute-done.2.other = f32[9,8,128]{2,1,0:T(8,128)S(1)} collective-permute-done((f32[9,8,128]{2,1,0:T(8,128)S(1)}, f32[9,8,128]{2,1,0:T(8,128)S(1)}, u32[]{:S(2)}, u32[]{:S(2)}) %collective-permute-start.2) | collective-permute-done | bytes 36896 | tf_op jit(solution)/shard_map/ppermute | solution.py:430
  33.0 0.1 shard_map.100
  33.1 12.2 %all_to_all.11.got = f32[32,16,128]{2,1,0:T(8,128)S(1)} all-to-all(f32[32,16,128]{2,1,0:T(8,128)S(1)} %shard_map.100), channel_id=1, replica_groups=mesh['x'=4,'zh'=2,'z1'=2,'z0'=2,'y'=4,'sp'=2] {'x','z0','y'}, dimensions={0} | all-to-all | bytes 524288 | tf_op jit(solution)/shard_map/all_to_all | solution.py:436
  45.3 0.0 copy-done.1
  45.3 0.7 %shard_map.101 = (f32[2,256,128]{2,1,0:T(8,128)S(1)}, f32[2,256,128]{2,1,0:T(8,128)S(1)}) custom-call(f32[32,16,128]{2,1,0:T(8,128)S(1)} %all_to_all.11.got, bf16[256,512]{1,0:T(8,128)(2,1)S(1)} %get-tuple-element.29.rows_t, bf16[384,128]{1,0:T(8,128)(2,1)S(1)} %copy-done.1), custom_call_target="tpu_custom_call" | custom-call | tf_op jit(solution)/shard_map/pallas_call | solution.py:380
  46.0 0.2 collective-permute-start.3
  46.2 1.4 %collective-permute-done.3 = f32[2,256,128]{2,1,0:T(8,128)S(1)} collective-permute-done((f32[2,256,128]{2,1,0:T(8,128)S(1)}, f32[2,256,128]{2,1,0:T(8,128)S(1)}, u32[]{:S(2)}, u32[]{:S(2)}) %collective-permute-start.3) | collective-permute-done | bytes 262176 | tf_op jit(solution)/shard_map/ppermute | solution.py:440
  47.6 0.7 %slice_add_fusion = (f32[1,256,128]{2,1,0:T(8,128)}, f32[1,256,128]{2,1,0:T(8,128)}) fusion(f32[2,256,128]{2,1,0:T(8,128)S(1)} %collective-permute-done.3, f32[2,256,128]{2,1,0:T(8,128)S(1)} %get-tuple-element.30), kind=kLoop, calls=%fused_computation | loop fusion | flops 65536 | bytes 786432 | tf_op jit(solution)/shard_map/add | solution.py:441
  (1 shorter events, 0.0 us)
Async XLA Ops:
  0.6 4.6 %copy-start = (bf16[768,128]{1,0:T(8,128)(2,1)S(1)}, bf16[768,128]{1,0:T(8,128)(2,1)}, u32[]{:S(2)}) copy-start(bf16[768,128]{1,0:T(8,128)(2,1)} %constant.16.clone.col) | copy-start | bytes 589828
  0.6 44.7 %copy-start.1 = (bf16[384,128]{1,0:T(8,128)(2,1)S(1)}, bf16[384,128]{1,0:T(8,128)(2,1)}, u32[]{:S(2)}) copy-start(bf16[384,128]{1,0:T(8,128)(2,1)} %constant.17.clone.col) | copy-start | bytes 294916
  0.7 4.6 %collective-permute-start = (f32[256,128]{1,0:T(8,128)}, f32[256,128]{1,0:T(8,128)S(1)}, u32[]{:S(2)}, u32[]{:S(2)}) collective-permute-start(f32[256,128]{1,0:T(8,128)} %bitcast.3), channel_id=1, source_target_pairs={{0,1},{1,0},{2,3},{3,2},{4,5},{5,4},{6,7},{7,6},{8,9},{9,8},{10,11... | collective-permute-start | bytes 393224 | tf_op jit(solution)/shard_map/ppermute | solution.py:401
  20.2 6.6 %collective-permute-start.1 = (f32[2,4,8,128]{3,2,1,0:T(8,128)S(1)}, f32[2,4,8,128]{3,2,1,0:T(8,128)S(1)}, u32[]{:S(2)}, u32[]{:S(2)}) collective-permute-start(f32[2,4,8,128]{3,2,1,0:T(8,128)S(1)} %get-tuple-element.24.own), channel_id=1, source_target_pairs={{0,17},{1,16},{16,1},{17,0},{2,19},{3,18},{18,3},{19,2},{4,21},{5,... | collective-permute-start | bytes 98312 | tf_op jit(solution)/shard_map/ppermute | solution.py:425
  26.9 6.2 %collective-permute-start.2 = (f32[9,8,128]{2,1,0:T(8,128)S(1)}, f32[9,8,128]{2,1,0:T(8,128)S(1)}, u32[]{:S(2)}, u32[]{:S(2)}) collective-permute-start(f32[9,8,128]{2,1,0:T(8,128)S(1)} %get-tuple-element.28.own), channel_id=1, source_target_pairs={{0,49},{1,48},{16,33},{17,32},{32,17},{33,16},{48,1},{49,0},{2,51}... | collective-permute-start | bytes 110600 | tf_op jit(solution)/shard_map/ppermute | solution.py:430
  46.0 1.6 %collective-permute-start.3 = (f32[2,256,128]{2,1,0:T(8,128)S(1)}, f32[2,256,128]{2,1,0:T(8,128)S(1)}, u32[]{:S(2)}, u32[]{:S(2)}) collective-permute-start(f32[2,256,128]{2,1,0:T(8,128)S(1)} %get-tuple-element.31), channel_id=1, source_target_pairs={{0,1},{1,0},{2,3},{3,2},{4,5},{5,4},{6,7},{7,6},{8,9},{9,8},{10,11... | collective-permute-start | bytes 786440 | tf_op jit(solution)/shard_map/ppermute | solution.py:440
